TPU v7x, 256 devices: a whole 4x4x8 slice. The times are simulated.
256 devices in a mesh: orb: 32 (over z, x), slab: 8 (over y, core).
Axes of the slice: x: 4, y: 4, z: 8, core: 2. Of those that a mesh axis runs over, the one named last changes fastest.
Arguments:
- orbitals: bfloat16 [32, 64, 64, 128], P('orb', 'slab'), may hold values from -6 to 6
- pair_table: int32 [1024, 3], P('orb'), may hold values from -1 to 31, as said below
Outputs:
- exchange_action: float32 [32, 64, 64, 128], P('orb', 'slab')
Inputs may be any that keep to these rules, and one draw needn't show every extreme that they name: `pair_table`: A live slot holds (m, n, s) with m <= n and s in 0, 1; an empty slot holds -1 in all three columns. A block of 32 slots has its live slots first. No (m, n, s) appears twice in the table. Exactly 528 slots are live, and the 32 blocks hold, in some order, k * 1 live slots for k = 1 to 32.
All inputs are finite; a program needn't handle non-finite values.
Results may differ from a plain program's by a relative error of at most 0.0003.
Values may be sent and summed in bfloat16 or wider, within the bound.
No kernel may reach another device: no remote copies, remote signals or barrier semaphores. Data moves between devices by JAX's collectives and lax.ppermute only.
A program may use at most 64 MiB of HBM per device.

v0:
```python
import math

import jax
import jax.numpy as jnp
from jax import lax
from jax.sharding import PartitionSpec as P

exchange_fraction = 0.25
cell_ratio = 8.0
slots_per_step = 4


def folded(values, grid_len):
    return jnp.minimum(values, grid_len - values).astype(jnp.float32)


def hartley(grid_len):
    rows_idx = jnp.arange(grid_len, dtype=jnp.int32)
    phase_int = rows_idx[:, None] * rows_idx[None, :] % grid_len
    angles = 2.0 * math.pi / grid_len * phase_int.astype(jnp.float32)
    return (jnp.cos(angles) + jnp.sin(angles)) / math.sqrt(grid_len)


def lane_turn(grid_len):
    index_range = jnp.arange(2 * grid_len, dtype=jnp.int32)
    return (index_range[None, :] == (index_range[:, None] + grid_len) % (2 * grid_len)).astype(
        jnp.float32
    )


def along_depth(field_in, depth_matrix):
    shape_in = field_in.shape
    flat_rows = field_in.reshape(-1, shape_in[-1])
    return jnp.dot(flat_rows, depth_matrix, precision=lax.Precision.HIGHEST).reshape(shape_in)


def along_rows(field_in, hartley_mat):
    return jnp.einsum("ky,bxyt->bxkt", hartley_mat, field_in, precision=lax.Precision.HIGHEST)


def along_planes(field_in, hartley_mat):
    return jnp.einsum("kx,bxyt->bkyt", hartley_mat, field_in, precision=lax.Precision.HIGHEST)


def coulomb(grid_len, slab_len, slab_index):
    planes_x = cell_ratio * folded(jnp.arange(grid_len, dtype=jnp.int32), grid_len)
    rows_y = folded(slab_index * slab_len + jnp.arange(slab_len, dtype=jnp.int32), grid_len)
    depth_z = folded(jnp.arange(2 * grid_len, dtype=jnp.int32) % grid_len, grid_len)
    scale_k = 2.0 * math.pi / grid_len * (2.0 * math.pi / grid_len)
    squared = scale_k * (
        planes_x[:, None, None] * planes_x[:, None, None]
        + rows_y[None, :, None] * rows_y[None, :, None]
        + depth_z[None, None, :] * depth_z[None, None, :]
    )
    safe_sq = jnp.where(squared > 0, squared, 1.0)
    return jnp.where(squared > 0, -exchange_fraction / safe_sq, 0.0)


def local(orbitals, pair_table):
    slab_len = orbitals.shape[1]
    grid_len = orbitals.shape[2]
    gathered = lax.all_gather(orbitals, "orb", axis=0, tiled=True)
    hartley_mat = hartley(grid_len)
    depth_matrix = jnp.kron(jnp.eye(2, dtype=jnp.float32), hartley_mat)
    turn_f32 = lane_turn(grid_len)
    ident_f32 = jnp.eye(2 * grid_len, dtype=jnp.float32)
    kernel = coulomb(grid_len, slab_len, lax.axis_index("slab"))

    def solve_planes(spectra):
        scaled = along_planes(spectra, hartley_mat) * kernel[None]
        returned = along_planes(scaled, hartley_mat)
        return lax.all_to_all(returned, "slab", split_axis=1, concat_axis=2, tiled=True)

    def one_block(block_index, totals):
        chosen = lax.dynamic_slice_in_dim(
            pair_table, block_index * slots_per_step, slots_per_step, 0
        )
        left_ids = chosen[:, 0]
        right_ids = chosen[:, 1]
        flipped = chosen[:, 2] == 1
        is_used = left_ids >= 0
        left_safe = jnp.maximum(left_ids, 0)
        right_safe = jnp.maximum(right_ids, 0)
        left_rows = gathered[left_safe].astype(jnp.float32)
        right_rows = gathered[right_safe].astype(jnp.float32)
        mixers = jnp.where(flipped[:, None, None], turn_f32[None], ident_f32[None])
        partner = jnp.einsum("bxyt,btu->bxyu", right_rows, mixers, precision=lax.Precision.HIGHEST)
        density = jnp.where(is_used[:, None, None, None], left_rows * partner, 0.0)
        spectra = along_rows(along_depth(density, depth_matrix), hartley_mat)
        solved = solve_planes(
            lax.all_to_all(spectra, "slab", split_axis=2, concat_axis=1, tiled=True)
        )
        potential = along_depth(along_rows(solved, hartley_mat), depth_matrix)
        first_term = potential * partner
        second_term = jnp.einsum(
            "bxyt,btu->bxyu", potential * left_rows, mixers, precision=lax.Precision.HIGHEST
        )
        second_term = jnp.where((left_ids != right_ids)[:, None, None, None], second_term, 0.0)
        totals = totals.at[left_safe].add(first_term)
        return totals.at[right_safe].add(second_term)

    block_count = pair_table.shape[0] // slots_per_step
    zeros_acc = jnp.zeros(gathered.shape, jnp.float32)
    totals = lax.fori_loop(0, block_count, one_block, zeros_acc)
    own_actions = lax.psum_scatter(totals, "orb", scatter_dimension=0, tiled=True)
    couples_own = own_actions.shape[0]
    flat_len = own_actions.shape[1] * own_actions.shape[2] * own_actions.shape[3]
    own_flat = own_actions.reshape(couples_own, flat_len)
    lane_of = jnp.arange(flat_len, dtype=jnp.int32) % (2 * grid_len) // grid_len
    lane_zero = (lane_of == 0).astype(jnp.float32)
    lane_one = 1.0 - lane_zero
    turned = along_depth(own_actions, turn_f32).reshape(couples_own, flat_len)
    variants = jnp.stack(
        [own_flat * lane_zero, turned * lane_one, turned * lane_zero, own_flat * lane_one], axis=1
    )
    variants = variants.reshape(4 * couples_own, flat_len)
    table_flat = gathered.reshape(gathered.shape[0], flat_len).astype(jnp.float32)
    cell_count = grid_len * grid_len * grid_len
    local_intersection = (
        lax.dot_general(
            table_flat, variants, (((1,), (1,)), ((), ())), precision=lax.Precision.HIGHEST
        )
        / cell_count
    )
    intersection = lax.psum(local_intersection, "slab")
    combined = lax.dot_general(
        intersection, table_flat, (((0,), (0,)), ((), ())), precision=lax.Precision.HIGHEST
    )
    combined = combined.reshape(couples_own, 4, flat_len)
    straight = combined[:, 0] * lane_zero + combined[:, 3] * lane_one
    crossed_in = (combined[:, 1] * lane_one + combined[:, 2] * lane_zero).reshape(own_actions.shape)
    crossed = along_depth(crossed_in, turn_f32).reshape(couples_own, flat_len)
    return (own_flat - straight - crossed).reshape(own_actions.shape)


def solution(mesh):
    placed = (P("orb", "slab", None, None), P("orb", None))
    return jax.shard_map(
        local, mesh=mesh, in_specs=placed, out_specs=P("orb", "slab", None, None), check_vma=False
    )
```

profile of v0, /device:TPU:1, one launch (start us, length us, event | category | flops | bytes accessed | tf_op | source)
XLA Modules:
  0.0 874.4 jit_solution(1319926327580846956)
XLA Ops:
  7.6 85.3 %all-gather.2.cloned.1.call-done = bf16[32,8,64,128]{3,2,1,0:T(8,128)(2,1)} async-done(((bf16[1,8,64,128]{3,2,1,0:T(8,128)(2,1)}), bf16[32,8,64,128]{3,2,1,0:T(8,128)(2,1)}) %all-gather.2.cloned.1.call-update) | async-done | bytes 4194320 | tf_op jit(solution)/shard_map/all_gather | solution.py:62
  97.2 513.1 %while.15 = (s32[]{:T(128)}, f32[32,8,64,128]{3,2,1,0:T(8,128)}, s32[32,3]{0,1:T(4,128)S(1)}, bf16[32,8,64,128]{3,2,1,0:T(8,128)(2,1)}, s32[128]{0:T(128)S(1)}, ...) while((s32[]{:T(128)}, f32[32,8,64,128]{3,2,1,0:T(8,128)}, ...), condition=%wide.region_3.4_spmd.clone.clone, body=%wide.region_0.3_spmd.clone.clone.sunk | while | flops 2419410944 | bytes 41643592 | solution.py:104
  107.9 7.6 all-to-all-start
  115.6 15.0 %all-to-all-done = f32[4,8,64,128]{3,1,0,2:T(8,128)S(1)} async-done(((f32[4,8,64,128]{3,1,0,2:T(8,128)}), f32[4,8,64,128]{3,1,0,2:T(8,128)S(1)}, u32[]{:S(2)}, u32[]{:S(2)}) %all-to-all-start) | async-done | bytes 1048608 | tf_op jit(solution)/shard_map/while/body/eval_jaxpr/all_to_all | solution.py:91
  135.3 4.3 all-to-all-start.1
  139.6 15.1 %all-to-all-done.1 = f32[4,64,8,128]{3,2,0,1:T(8,128)S(1)} async-done(((f32[4,64,8,128]{3,2,0,1:T(8,128)}), f32[4,64,8,128]{3,2,0,1:T(8,128)S(1)}, u32[]{:S(2)}, u32[]{:S(2)}) %all-to-all-start.1) | async-done | bytes 1048608 | tf_op jit(solution)/shard_map/while/body/eval_jaxpr/all_to_all | solution.py:72
  179.4 15.0 %all-to-all-done = f32[4,8,64,128]{3,1,0,2:T(8,128)S(1)} async-done(((f32[4,8,64,128]{3,1,0,2:T(8,128)}), f32[4,8,64,128]{3,1,0,2:T(8,128)S(1)}, u32[]{:S(2)}, u32[]{:S(2)}) %all-to-all-start) | async-done | bytes 1048608 | tf_op jit(solution)/shard_map/while/body/eval_jaxpr/all_to_all | solution.py:91
  203.5 15.1 %all-to-all-done.1 = f32[4,64,8,128]{3,2,0,1:T(8,128)S(1)} async-done(((f32[4,64,8,128]{3,2,0,1:T(8,128)}), f32[4,64,8,128]{3,2,0,1:T(8,128)S(1)}, u32[]{:S(2)}, u32[]{:S(2)}) %all-to-all-start.1) | async-done | bytes 1048608 | tf_op jit(solution)/shard_map/while/body/eval_jaxpr/all_to_all | solution.py:72
  243.3 15.0 %all-to-all-done = f32[4,8,64,128]{3,1,0,2:T(8,128)S(1)} async-done(((f32[4,8,64,128]{3,1,0,2:T(8,128)}), f32[4,8,64,128]{3,1,0,2:T(8,128)S(1)}, u32[]{:S(2)}, u32[]{:S(2)}) %all-to-all-start) | async-done | bytes 1048608 | tf_op jit(solution)/shard_map/while/body/eval_jaxpr/all_to_all | solution.py:91
  267.3 15.1 %all-to-all-done.1 = f32[4,64,8,128]{3,2,0,1:T(8,128)S(1)} async-done(((f32[4,64,8,128]{3,2,0,1:T(8,128)}), f32[4,64,8,128]{3,2,0,1:T(8,128)S(1)}, u32[]{:S(2)}, u32[]{:S(2)}) %all-to-all-start.1) | async-done | bytes 1048608 | tf_op jit(solution)/shard_map/while/body/eval_jaxpr/all_to_all | solution.py:72
  307.2 15.0 %all-to-all-done = f32[4,8,64,128]{3,1,0,2:T(8,128)S(1)} async-done(((f32[4,8,64,128]{3,1,0,2:T(8,128)}), f32[4,8,64,128]{3,1,0,2:T(8,128)S(1)}, u32[]{:S(2)}, u32[]{:S(2)}) %all-to-all-start) | async-done | bytes 1048608 | tf_op jit(solution)/shard_map/while/body/eval_jaxpr/all_to_all | solution.py:91
  331.2 15.1 %all-to-all-done.1 = f32[4,64,8,128]{3,2,0,1:T(8,128)S(1)} async-done(((f32[4,64,8,128]{3,2,0,1:T(8,128)}), f32[4,64,8,128]{3,2,0,1:T(8,128)S(1)}, u32[]{:S(2)}, u32[]{:S(2)}) %all-to-all-start.1) | async-done | bytes 1048608 | tf_op jit(solution)/shard_map/while/body/eval_jaxpr/all_to_all | solution.py:72
  370.9 15.0 %all-to-all-done = f32[4,8,64,128]{3,1,0,2:T(8,128)S(1)} async-done(((f32[4,8,64,128]{3,1,0,2:T(8,128)}), f32[4,8,64,128]{3,1,0,2:T(8,128)S(1)}, u32[]{:S(2)}, u32[]{:S(2)}) %all-to-all-start) | async-done | bytes 1048608 | tf_op jit(solution)/shard_map/while/body/eval_jaxpr/all_to_all | solution.py:91
  394.9 15.1 %all-to-all-done.1 = f32[4,64,8,128]{3,2,0,1:T(8,128)S(1)} async-done(((f32[4,64,8,128]{3,2,0,1:T(8,128)}), f32[4,64,8,128]{3,2,0,1:T(8,128)S(1)}, u32[]{:S(2)}, u32[]{:S(2)}) %all-to-all-start.1) | async-done | bytes 1048608 | tf_op jit(solution)/shard_map/while/body/eval_jaxpr/all_to_all | solution.py:72
  434.5 15.0 %all-to-all-done = f32[4,8,64,128]{3,1,0,2:T(8,128)S(1)} async-done(((f32[4,8,64,128]{3,1,0,2:T(8,128)}), f32[4,8,64,128]{3,1,0,2:T(8,128)S(1)}, u32[]{:S(2)}, u32[]{:S(2)}) %all-to-all-start) | async-done | bytes 1048608 | tf_op jit(solution)/shard_map/while/body/eval_jaxpr/all_to_all | solution.py:91
  458.5 15.1 %all-to-all-done.1 = f32[4,64,8,128]{3,2,0,1:T(8,128)S(1)} async-done(((f32[4,64,8,128]{3,2,0,1:T(8,128)}), f32[4,64,8,128]{3,2,0,1:T(8,128)S(1)}, u32[]{:S(2)}, u32[]{:S(2)}) %all-to-all-start.1) | async-done | bytes 1048608 | tf_op jit(solution)/shard_map/while/body/eval_jaxpr/all_to_all | solution.py:72
  498.2 15.0 %all-to-all-done = f32[4,8,64,128]{3,1,0,2:T(8,128)S(1)} async-done(((f32[4,8,64,128]{3,1,0,2:T(8,128)}), f32[4,8,64,128]{3,1,0,2:T(8,128)S(1)}, u32[]{:S(2)}, u32[]{:S(2)}) %all-to-all-start) | async-done | bytes 1048608 | tf_op jit(solution)/shard_map/while/body/eval_jaxpr/all_to_all | solution.py:91
  522.2 15.1 %all-to-all-done.1 = f32[4,64,8,128]{3,2,0,1:T(8,128)S(1)} async-done(((f32[4,64,8,128]{3,2,0,1:T(8,128)}), f32[4,64,8,128]{3,2,0,1:T(8,128)S(1)}, u32[]{:S(2)}, u32[]{:S(2)}) %all-to-all-start.1) | async-done | bytes 1048608 | tf_op jit(solution)/shard_map/while/body/eval_jaxpr/all_to_all | solution.py:72
  561.8 15.0 %all-to-all-done = f32[4,8,64,128]{3,1,0,2:T(8,128)S(1)} async-done(((f32[4,8,64,128]{3,1,0,2:T(8,128)}), f32[4,8,64,128]{3,1,0,2:T(8,128)S(1)}, u32[]{:S(2)}, u32[]{:S(2)}) %all-to-all-start) | async-done | bytes 1048608 | tf_op jit(solution)/shard_map/while/body/eval_jaxpr/all_to_all | solution.py:91
  585.8 15.1 %all-to-all-done.1 = f32[4,64,8,128]{3,2,0,1:T(8,128)S(1)} async-done(((f32[4,64,8,128]{3,2,0,1:T(8,128)}), f32[4,64,8,128]{3,2,0,1:T(8,128)S(1)}, u32[]{:S(2)}, u32[]{:S(2)}) %all-to-all-start.1) | async-done | bytes 1048608 | tf_op jit(solution)/shard_map/while/body/eval_jaxpr/all_to_all | solution.py:72
  610.4 220.9 %reduce-scatter.2.cloned.1.call-done = f32[1,8,64,128]{3,2,1,0:T(8,128)} async-done(((f32[32,8,64,128]{3,2,1,0:T(8,128)}), f32[1,8,64,128]{3,2,1,0:T(8,128)}) %reduce-scatter.2.cloned.1.call-update) | async-done | bytes 262160 | tf_op jit(solution)/shard_map/reduce_scatter | solution.py:105
  835.0 8.1 fusion.76
  843.1 16.5 %psum.7 = f32[32,4]{0,1:T(4,128)S(1)} all-reduce(f32[32,4]{0,1:T(4,128)S(1)} %fusion.76), channel_id=1, replica_groups=mesh['orb'=32,'slab'=8] {'slab'}, use_global_device_ids=true, to_apply=%region_5.6 | all-reduce | flops 128 | bytes 1024 | tf_op jit(solution)/shard_map/psum | solution.py:125
  859.5 5.7 convolution_bitcast_fusion.4
  (219 shorter events, 270.9 us)
Async XLA Ops:
  6.5 86.4 %all-gather.2.cloned.1.call-start = ((), (), s32[]{:S(2)}) async-start(), calls=%async_computation.3 | async-start | bytes 4325376 | tf_op jit(solution)/shard_map/all_gather | solution.py:62
  7.3 824.0 %reduce-scatter.2.cloned.1.call-start = ((), (), s32[]{:S(2)}) async-start(), calls=%async_computation.4 | async-start | bytes 8650752 | tf_op jit(solution)/shard_map/reduce_scatter | solution.py:105
  7.6 89.6 %copy-start.1 = (s32[32,3]{0,1:T(4,128)S(1)}, s32[32,3]{0,1:T(4,128)}, u32[]{:S(2)}) copy-start(s32[32,3]{0,1:T(4,128)} %param.5) | copy-start | bytes 1156
  107.9 22.7 %all-to-all-start = ((f32[4,8,64,128]{3,1,0,2:T(8,128)}), f32[4,8,64,128]{3,1,0,2:T(8,128)S(1)}, u32[]{:S(2)}, u32[]{:S(2)}) async-start(f32[4,8,64,128]{3,1,0,2:T(8,128)} %copy.46), calls=%async_computation | async-start | bytes 2097152 | tf_op jit(solution)/shard_map/while/body/eval_jaxpr/all_to_all | solution.py:91
  135.3 19.5 %all-to-all-start.1 = ((f32[4,64,8,128]{3,2,0,1:T(8,128)}), f32[4,64,8,128]{3,2,0,1:T(8,128)S(1)}, u32[]{:S(2)}, u32[]{:S(2)}) async-start(f32[4,64,8,128]{3,2,0,1:T(8,128)} %copy.48), calls=%async_computation.1 | async-start | bytes 2097152 | tf_op jit(solution)/shard_map/while/body/eval_jaxpr/all_to_all | solution.py:72
  175.0 19.4 %all-to-all-start = ((f32[4,8,64,128]{3,1,0,2:T(8,128)}), f32[4,8,64,128]{3,1,0,2:T(8,128)S(1)}, u32[]{:S(2)}, u32[]{:S(2)}) async-start(f32[4,8,64,128]{3,1,0,2:T(8,128)} %copy.46), calls=%async_computation | async-start | bytes 2097152 | tf_op jit(solution)/shard_map/while/body/eval_jaxpr/all_to_all | solution.py:91
  199.1 19.5 %all-to-all-start.1 = ((f32[4,64,8,128]{3,2,0,1:T(8,128)}), f32[4,64,8,128]{3,2,0,1:T(8,128)S(1)}, u32[]{:S(2)}, u32[]{:S(2)}) async-start(f32[4,64,8,128]{3,2,0,1:T(8,128)} %copy.48), calls=%async_computation.1 | async-start | bytes 2097152 | tf_op jit(solution)/shard_map/while/body/eval_jaxpr/all_to_all | solution.py:72
  238.8 19.4 %all-to-all-start = ((f32[4,8,64,128]{3,1,0,2:T(8,128)}), f32[4,8,64,128]{3,1,0,2:T(8,128)S(1)}, u32[]{:S(2)}, u32[]{:S(2)}) async-start(f32[4,8,64,128]{3,1,0,2:T(8,128)} %copy.46), calls=%async_computation | async-start | bytes 2097152 | tf_op jit(solution)/shard_map/while/body/eval_jaxpr/all_to_all | solution.py:91
  263.0 19.5 %all-to-all-start.1 = ((f32[4,64,8,128]{3,2,0,1:T(8,128)}), f32[4,64,8,128]{3,2,0,1:T(8,128)S(1)}, u32[]{:S(2)}, u32[]{:S(2)}) async-start(f32[4,64,8,128]{3,2,0,1:T(8,128)} %copy.48), calls=%async_computation.1 | async-start | bytes 2097152 | tf_op jit(solution)/shard_map/while/body/eval_jaxpr/all_to_all | solution.py:72
  302.7 19.5 %all-to-all-start = ((f32[4,8,64,128]{3,1,0,2:T(8,128)}), f32[4,8,64,128]{3,1,0,2:T(8,128)S(1)}, u32[]{:S(2)}, u32[]{:S(2)}) async-start(f32[4,8,64,128]{3,1,0,2:T(8,128)} %copy.46), calls=%async_computation | async-start | bytes 2097152 | tf_op jit(solution)/shard_map/while/body/eval_jaxpr/all_to_all | solution.py:91
  326.9 19.4 %all-to-all-start.1 = ((f32[4,64,8,128]{3,2,0,1:T(8,128)}), f32[4,64,8,128]{3,2,0,1:T(8,128)S(1)}, u32[]{:S(2)}, u32[]{:S(2)}) async-start(f32[4,64,8,128]{3,2,0,1:T(8,128)} %copy.48), calls=%async_computation.1 | async-start | bytes 2097152 | tf_op jit(solution)/shard_map/while/body/eval_jaxpr/all_to_all | solution.py:72
  366.4 19.4 %all-to-all-start = ((f32[4,8,64,128]{3,1,0,2:T(8,128)}), f32[4,8,64,128]{3,1,0,2:T(8,128)S(1)}, u32[]{:S(2)}, u32[]{:S(2)}) async-start(f32[4,8,64,128]{3,1,0,2:T(8,128)} %copy.46), calls=%async_computation | async-start | bytes 2097152 | tf_op jit(solution)/shard_map/while/body/eval_jaxpr/all_to_all | solution.py:91
  390.6 19.4 %all-to-all-start.1 = ((f32[4,64,8,128]{3,2,0,1:T(8,128)}), f32[4,64,8,128]{3,2,0,1:T(8,128)S(1)}, u32[]{:S(2)}, u32[]{:S(2)}) async-start(f32[4,64,8,128]{3,2,0,1:T(8,128)} %copy.48), calls=%async_computation.1 | async-start | bytes 2097152 | tf_op jit(solution)/shard_map/while/body/eval_jaxpr/all_to_all | solution.py:72
  430.0 19.4 %all-to-all-start = ((f32[4,8,64,128]{3,1,0,2:T(8,128)}), f32[4,8,64,128]{3,1,0,2:T(8,128)S(1)}, u32[]{:S(2)}, u32[]{:S(2)}) async-start(f32[4,8,64,128]{3,1,0,2:T(8,128)} %copy.46), calls=%async_computation | async-start | bytes 2097152 | tf_op jit(solution)/shard_map/while/body/eval_jaxpr/all_to_all | solution.py:91
  454.2 19.5 %all-to-all-start.1 = ((f32[4,64,8,128]{3,2,0,1:T(8,128)}), f32[4,64,8,128]{3,2,0,1:T(8,128)S(1)}, u32[]{:S(2)}, u32[]{:S(2)}) async-start(f32[4,64,8,128]{3,2,0,1:T(8,128)} %copy.48), calls=%async_computation.1 | async-start | bytes 2097152 | tf_op jit(solution)/shard_map/while/body/eval_jaxpr/all_to_all | solution.py:72
  493.7 19.4 %all-to-all-start = ((f32[4,8,64,128]{3,1,0,2:T(8,128)}), f32[4,8,64,128]{3,1,0,2:T(8,128)S(1)}, u32[]{:S(2)}, u32[]{:S(2)}) async-start(f32[4,8,64,128]{3,1,0,2:T(8,128)} %copy.46), calls=%async_computation | async-start | bytes 2097152 | tf_op jit(solution)/shard_map/while/body/eval_jaxpr/all_to_all | solution.py:91
  517.8 19.5 %all-to-all-start.1 = ((f32[4,64,8,128]{3,2,0,1:T(8,128)}), f32[4,64,8,128]{3,2,0,1:T(8,128)S(1)}, u32[]{:S(2)}, u32[]{:S(2)}) async-start(f32[4,64,8,128]{3,2,0,1:T(8,128)} %copy.48), calls=%async_computation.1 | async-start | bytes 2097152 | tf_op jit(solution)/shard_map/while/body/eval_jaxpr/all_to_all | solution.py:72
  557.3 19.4 %all-to-all-start = ((f32[4,8,64,128]{3,1,0,2:T(8,128)}), f32[4,8,64,128]{3,1,0,2:T(8,128)S(1)}, u32[]{:S(2)}, u32[]{:S(2)}) async-start(f32[4,8,64,128]{3,1,0,2:T(8,128)} %copy.46), calls=%async_computation | async-start | bytes 2097152 | tf_op jit(solution)/shard_map/while/body/eval_jaxpr/all_to_all | solution.py:91
  581.5 19.5 %all-to-all-start.1 = ((f32[4,64,8,128]{3,2,0,1:T(8,128)}), f32[4,64,8,128]{3,2,0,1:T(8,128)S(1)}, u32[]{:S(2)}, u32[]{:S(2)}) async-start(f32[4,64,8,128]{3,2,0,1:T(8,128)} %copy.48), calls=%async_computation.1 | async-start | bytes 2097152 | tf_op jit(solution)/shard_map/while/body/eval_jaxpr/all_to_all | solution.py:72
  843.1 22.9 %copy-start = (f32[1,8,64,128]{3,2,1,0:T(8,128)S(1)}, f32[1,8,64,128]{3,2,1,0:T(8,128)}, u32[]{:S(2)}) copy-start(f32[1,8,64,128]{3,2,1,0:T(8,128)} %reduce-scatter.2.cloned.1.call-done) | copy-start | bytes 786436
Sparse Core Ops, SparseCore 0:
  9.9 82.9 all-gather.1
  610.5 220.7 reduce-scatter.1
where the time goes:
time: 876 us; the launch traced here: 874 us
  waiting for transfers between devices  548 us (63%)
  matrix products  85.2 us (10%)
  local copies, waits for them, and re-layouts  83.2 us (9%)
  starting transfers between devices  72.6 us (8%)
  other arithmetic  54.9 us (6%)
  blocking collectives  16.5 us (2%)
  between operations  13.5 us (2%)
    reduce_scatter x1, waiting for transfers between devices, local(): lax.psum_scatter(totals, 'orb', scatter_dimension=0, tiled=True)  221 us
    all_to_all x8, waiting for transfers between devices, solve_planes(): lax.all_to_all(returned, 'slab', split_axis=1, concat_axis=2, tiled=True)  121 us
    all_to_all x8, waiting for transfers between devices, one_block(): lax.all_to_all(spectra, 'slab', split_axis=2, concat_axis=1, tiled=True)  120 us
    all_gather x1, waiting for transfers between devices, local(): gathered = lax.all_gather(orbitals, 'orb', axis=0, tiled=True)  85.3 us
    all_to_all x8, starting transfers between devices, one_block(): lax.all_to_all(spectra, 'slab', split_axis=2, concat_axis=1, tiled=True)  37.9 us
    all_to_all x8, starting transfers between devices, solve_planes(): lax.all_to_all(returned, 'slab', split_axis=1, concat_axis=2, tiled=True)  34.6 us
    scatter-add x8, other arithmetic, one_block(): totals = totals.at[left_safe].add(first_term)  24.8 us
    scatter-add x8, other arithmetic, one_block(): return totals.at[right_safe].add(second_term)  24.7 us
  transfers between devices with their start and end apart: 18, of which 18 were waited for; matrix products, arithmetic and copies ran while one was open for 0% of the time, Pallas kernels for 0%

commit v1 on v0

v1 whole, which is shorter than its diff:
```python
import functools
import math

import jax
import jax.numpy as jnp
import ml_dtypes
import numpy as np
from jax import lax
from jax.experimental import pallas as pl
from jax.experimental.pallas import tpu as pltpu
from jax.sharding import Mesh
from jax.sharding import PartitionSpec as P

G = 64
ROWS = 2048
CHUNK = 256
KY_STEP = 4
NZ, NX, NY = 8, 4, 4
COUPLES = 32
CELLS = G * G * G
exchange_fraction = 0.25
cell_ratio = 8.0
f32, bf16 = jnp.float32, jnp.bfloat16


def split_np(mat):
    high = mat.astype(ml_dtypes.bfloat16)
    low = (mat - high.astype(np.float64)).astype(ml_dtypes.bfloat16)
    return high, low


def plane_order():
    r = np.arange(32)
    return [16 * (r // 8) + 8 * h + r % 8 for h in (0, 1)]


def weights():
    idx = np.arange(G)
    angles = 2.0 * np.pi / G * (idx[:, None] * idx[None, :] % G)
    hart = (np.cos(angles) + np.sin(angles)) / math.sqrt(G)
    high, low = split_np(np.kron(np.eye(2), hart))
    zero = np.zeros_like(high)
    w_depth = np.block([[high, low], [high, zero]])
    w_rows = np.block([[high, high], [low, zero]])
    s0, s1 = plane_order()
    mix = np.block(
        [
            [hart[np.ix_(s0, s0)], hart[np.ix_(s0, s1)]],
            [hart[np.ix_(s1, s1)], hart[np.ix_(s1, s0)]],
        ]
    )
    high, low = split_np(mix)
    w_planes = np.block([[high, high], [low, np.zeros_like(high)]])
    return w_depth, w_rows, w_planes


def coulomb():
    def folded(v):
        return jnp.minimum(v, G - v).astype(f32)

    lane = lax.broadcasted_iota(jnp.int32, (G, 32, 128), 2)
    row = lax.broadcasted_iota(jnp.int32, (G, 32, 128), 1)
    ky = folded(lax.broadcasted_iota(jnp.int32, (G, 32, 128), 0))
    kx = cell_ratio * folded(16 * (row // 8) + 8 * (lane // G) + row % 8)
    kz = folded(lane % G)
    scale = (2.0 * math.pi / G) * (2.0 * math.pi / G)
    squared = scale * (kx * kx + ky * ky + kz * kz)
    safe = jnp.where(squared > 0, squared, 1.0)
    return jnp.where(squared > 0, -exchange_fraction / safe, 0.0)


def assign_kernel(me_ref, code_ref, out_ref, load_ref):
    me = me_ref[0]

    def clear(i, carry):
        load_ref[i] = 0
        return carry

    lax.fori_loop(0, NZ * NX * NY, clear, 0)
    for i in range(17):
        out_ref[i] = 0

    def one_block(b, count):
        def live(state):
            s, _ = state
            return (s < 32) & (code_ref[b, jnp.minimum(s, 31)] >= 0)

        def step(state):
            s, cnt = state
            code = code_ref[b, s]
            m = code & 31
            n = (code >> 5) & 31
            flip = code >> 10
            mz, mx, nz, nx = m >> 2, m & 3, n >> 2, n & 3
            first = mz * 16 + nx * 4 + (nz >> 1)
            second = nz * 16 + mx * 4 + (mz >> 1)
            load_a = load_ref[first]
            load_b = load_ref[second]
            use_a = load_a <= load_b
            chip = jnp.where(use_a, first, second)
            load_ref[chip] = jnp.where(use_a, load_a, load_b) + 1
            task_a = mx + 4 * (nz & 1)
            task_b = nx + 4 * (mz & 1)
            task = jnp.where(use_a, task_a, task_b) + 8 * flip + 16 * (m == n).astype(jnp.int32)
            mine = chip == me

            @pl.when(mine)
            def _():
                out_ref[1 + cnt] = task

            return s + 1, cnt + mine.astype(jnp.int32)

        return lax.while_loop(live, step, (0, count))[1]

    out_ref[0] = lax.fori_loop(0, 32, one_block, 0)


def split(value):
    high = value.astype(bf16)
    return high, (value - high.astype(f32)).astype(bf16)


def depth_transform(value, w_depth):
    high, low = split(value)
    out = jnp.dot(jnp.concatenate([high, low], axis=1), w_depth, preferred_element_type=f32)
    return out[:, :128] + out[:, 128:]


def rows_transform(value, w_rows):
    high, low = split(value)
    half = CHUNK // 2
    top = jnp.concatenate([high[:half], high[half:]], axis=1)
    bottom = jnp.concatenate([low[:half], low[half:]], axis=1)
    out = jnp.dot(w_rows, jnp.concatenate([top, bottom], axis=0), preferred_element_type=f32)
    out = out[:half] + out[half:]
    return jnp.concatenate([out[:, :128], out[:, 128:]], axis=0)


def planes_transform(value, w_planes, low_lanes):
    turned = jnp.concatenate(
        [pltpu.roll(value[:, j * 128 : (j + 1) * 128], G, 1) for j in range(KY_STEP)], axis=1
    )
    vh, vl = split(value)
    th, tl = split(turned)
    out = jnp.dot(w_planes, jnp.concatenate([vh, th, vl, tl], axis=0), preferred_element_type=f32)
    out = out[:64] + out[64:]
    return jnp.where(low_lanes, out[:32], out[32:])


def pairs_kernel(lane_ref, tasks_ref, left_ref, right_ref, wz_ref, wy_ref, wx_ref, kern_ref, lacc_ref, racc_ref, t_ref):
    def clear(i, carry):
        rows = pl.ds(pl.multiple_of(i * CHUNK, CHUNK), CHUNK)
        for k in range(4):
            lacc_ref[k, rows] = jnp.zeros((CHUNK, 128), f32)
            racc_ref[k, rows] = jnp.zeros((CHUNK, 128), f32)
        return carry

    lax.fori_loop(0, ROWS // CHUNK, clear, 0)
    lane = lane_ref[0]
    low_lanes = lax.broadcasted_iota(jnp.int32, (32, KY_STEP * 128), 1) % 128 < G

    def one_task(t, carry):
        task = tasks_ref[1 + t]
        a = task & 3
        flip = (task >> 3) & 1
        b = (lane ^ flip) * 2 + ((task >> 2) & 1)
        second = 1.0 - (task >> 4).astype(f32)

        def forward(i, c):
            rows = pl.ds(pl.multiple_of(i * CHUNK, CHUNK), CHUNK)
            rho = left_ref[a, rows].astype(f32) * right_ref[b, rows].astype(f32)
            t_ref[rows] = rows_transform(depth_transform(rho, wz_ref[...]), wy_ref[...])
            return c

        lax.fori_loop(0, ROWS // CHUNK, forward, 0, unroll=2)

        def middle(i, c):
            first = i * KY_STEP
            value = jnp.concatenate(
                [t_ref[pl.ds(first + j, 32, stride=G)] for j in range(KY_STEP)], axis=1
            )
            kern = jnp.concatenate([kern_ref[first + j] for j in range(KY_STEP)], axis=1)
            value = planes_transform(value, wx_ref[...], low_lanes) * kern
            value = planes_transform(value, wx_ref[...], low_lanes)
            for j in range(KY_STEP):
                t_ref[pl.ds(first + j, 32, stride=G)] = value[:, j * 128 : (j + 1) * 128]
            return c

        lax.fori_loop(0, G // KY_STEP, middle, 0, unroll=2)

        def backward(i, c):
            rows = pl.ds(pl.multiple_of(i * CHUNK, CHUNK), CHUNK)
            v = depth_transform(rows_transform(t_ref[rows], wy_ref[...]), wz_ref[...])
            lacc_ref[a, rows] += v * right_ref[b, rows].astype(f32)
            racc_ref[b, rows] += (v * second) * left_ref[a, rows].astype(f32)
            return c

        lax.fori_loop(0, ROWS // CHUNK, backward, 0, unroll=2)
        return carry

    lax.fori_loop(0, tasks_ref[0], one_task, 0)


def overlap_kernel(x_ref, phi_ref, out_ref, turned_ref):
    for i in range(8):
        turned_ref[pl.ds(i * 64, 64)] = pltpu.roll(x_ref[pl.ds(i * 64, 64)], G, 1)

    def one(o, carry):
        same = jnp.zeros((64, 128), f32)
        cross = jnp.zeros((64, 128), f32)
        for i in range(8):
            rows = pl.ds(i * 64, 64)
            phi = phi_ref[o, rows].astype(f32)
            same = same + phi * x_ref[rows]
            cross = cross + phi * turned_ref[rows]
        out_ref[o, 0:1] = jnp.sum(same, axis=0, keepdims=True)
        out_ref[o, 1:2] = jnp.sum(cross, axis=0, keepdims=True)
        return carry

    lax.fori_loop(0, COUPLES, one, 0)


def project_kernel(x_ref, phi_ref, over_ref, out_ref, coef_ref):
    lane = lax.broadcasted_iota(jnp.int32, (COUPLES, 128), 1)
    for k in range(2):
        part = over_ref[:, k]
        low = jnp.sum(jnp.where(lane < G, part, 0.0), axis=1, keepdims=True)
        high = jnp.sum(jnp.where(lane < G, 0.0, part), axis=1, keepdims=True)
        coef_ref[k] = jnp.where(lane < G, low, high) / CELLS

    def one(i, carry):
        rows = pl.ds(pl.multiple_of(i * 64, 64), 64)
        same = jnp.zeros((64, 128), f32)
        cross = jnp.zeros((64, 128), f32)
        for o in range(COUPLES):
            phi = phi_ref[o, rows].astype(f32)
            same = same + phi * coef_ref[0, o : o + 1]
            cross = cross + phi * coef_ref[1, o : o + 1]
        out_ref[rows] = x_ref[rows] - same - pltpu.roll(cross, G, 1)
        return carry

    lax.fori_loop(0, 8, one, 0)


def vmem_specs(n):
    return [pl.BlockSpec(memory_space=pltpu.VMEM)] * n


def smem_specs(n):
    return [pl.BlockSpec(memory_space=pltpu.SMEM)] * n


def lane_exchange(mine, core):
    other = lax.ppermute(mine, "core", [(0, 1), (1, 0)])
    lane = lax.broadcasted_iota(jnp.int32, mine.shape, mine.ndim - 1)
    return jnp.where((lane < G) == (core == 0), mine, jnp.roll(other, G, axis=-1))


def moves():
    return [(z * NY + y, ((z & 1) * NY + y) * NY + (z >> 1)) for z in range(NZ) for y in range(NY)]


def local(orbitals, pair_table):
    z, x, y, core = (lax.axis_index(a) for a in ("z", "x", "y", "core"))
    mine = orbitals[0]
    live = pair_table[:, 0] >= 0
    code = jnp.where(live, pair_table[:, 0] + 32 * pair_table[:, 1] + 1024 * pair_table[:, 2], -1)
    codes = lax.all_gather(code[None], ("z", "x"), axis=0, tiled=True)
    own = lane_exchange(mine, core)
    left = lax.all_gather(lax.all_gather(own, "y", axis=0, tiled=True), "x", axis=0, tiled=True)
    right = lax.all_gather(lax.ppermute(own, ("z", "y"), moves()), "z", axis=0, tiled=True)
    right = lax.all_gather(right, "core", axis=0, tiled=True)
    phi_all = lax.all_gather(orbitals, ("z", "x"), axis=0, tiled=True)

    me = (z * 16 + x * 4 + y).astype(jnp.int32).reshape(1)
    tasks = pl.pallas_call(
        assign_kernel,
        out_shape=jax.ShapeDtypeStruct((17,), jnp.int32),
        in_specs=smem_specs(2),
        out_specs=pl.BlockSpec(memory_space=pltpu.SMEM),
        scratch_shapes=[pltpu.SMEM((NZ * NX * NY,), jnp.int32)],
        name="assign",
    )(me, codes)

    w_depth, w_rows, w_planes = (jnp.asarray(w) for w in weights())
    acc = jax.ShapeDtypeStruct((4, ROWS, 128), f32)
    lacc, racc = pl.pallas_call(
        pairs_kernel,
        out_shape=(acc, acc),
        in_specs=smem_specs(2) + vmem_specs(6),
        out_specs=tuple(vmem_specs(2)),
        scratch_shapes=[pltpu.VMEM((ROWS, 128), f32)],
        compiler_params=pltpu.CompilerParams(vmem_limit_bytes=48 * 1024 * 1024),
        name="pairs",
    )(
        core.astype(jnp.int32).reshape(1),
        tasks,
        left.reshape(4, ROWS, 128),
        right.reshape(4, ROWS, 128),
        w_depth,
        w_rows,
        w_planes,
        coulomb(),
    )

    from_left = lax.psum_scatter(lacc.reshape(NX, NY, 512, 128), "x", scatter_dimension=0, tiled=True)
    from_left = lax.psum_scatter(from_left[0], "y", scatter_dimension=0, tiled=True)
    from_right = lax.psum_scatter(racc.reshape(2, NZ, 512, 128), "core", scatter_dimension=0, tiled=True)
    from_right = lax.psum_scatter(from_right[0], "z", scatter_dimension=0, tiled=True)
    from_right = lax.ppermute(from_right, ("z", "y"), [(d, s) for s, d in moves()])
    action = lane_exchange((from_left + from_right)[0], core)

    phi_rows = phi_all.reshape(COUPLES, 512, 128)
    over = pl.pallas_call(
        overlap_kernel,
        out_shape=jax.ShapeDtypeStruct((COUPLES, 2, 128), f32),
        in_specs=vmem_specs(2),
        out_specs=vmem_specs(1)[0],
        scratch_shapes=[pltpu.VMEM((512, 128), f32)],
        name="overlap",
    )(action, phi_rows)
    over = lax.psum(over, ("y", "core"))
    out = pl.pallas_call(
        project_kernel,
        out_shape=jax.ShapeDtypeStruct((512, 128), f32),
        in_specs=vmem_specs(3),
        out_specs=vmem_specs(1)[0],
        scratch_shapes=[pltpu.VMEM((2, COUPLES, 128), f32)],
        name="project",
    )(action, phi_rows, over)
    return out.reshape(1, 8, G, 128)


def solution(mesh):
    grid = Mesh(mesh.devices.reshape(NZ, NX, NY, 2), ("z", "x", "y", "core"))
    placed = (P(("z", "x"), ("y", "core"), None, None), P(("z", "x"), None))
    return jax.shard_map(
        local,
        mesh=grid,
        in_specs=placed,
        out_specs=P(("z", "x"), ("y", "core"), None, None),
        check_vma=False,
    )
```

time: 876 us -> 402 us (0.46)
  waiting for transfers between devices: 548 us -> 214 us
  matrix products: 85.2 us -> 0 us
  Pallas kernels: 0 us -> 85 us
  local copies, waits for them, and re-layouts: 83.2 us -> 6.69 us
  starting transfers between devices: 72.6 us -> 8.91 us
  other arithmetic: 54.9 us -> 4.34 us
  blocking collectives: 16.5 us -> 59.8 us
    all_to_all x16 -> x0, waiting for transfers between devices: 241 us -> none  [the longest x8 121 us: solve_planes(): lax.all_to_all(returned, 'slab', split_axis=1, concat_axis=2, tiled=True)]
    dot_general x68 -> x0, matrix products: 85.2 us -> none  [the longest x16 19.6 us: along_planes(): jnp.einsum('kx,bxyt->bkyt', hartley_mat, field_in, precision=lax.Precisio...]
    pallas_call x0 -> x4, Pallas kernels: none -> 85 us  [the longest x1 56.5 us: local(): pl.pallas_call(pairs_kernel, out_shape=(acc, acc), in_specs=smem_specs(2)...]
    all_to_all x16 -> x0, starting transfers between devices: 72.5 us -> none  [the longest x8 37.9 us: one_block(): lax.all_to_all(spectra, 'slab', split_axis=2, concat_axis=1, tiled=True)]
    reduce_scatter x1 -> x4, waiting for transfers between devices: 221 us -> 152 us  [the longest x1 52.8 us: local(): lax.psum_scatter(lacc.reshape(NX, NY, 512, 128), 'x', scatter_dimension=0...]
    scatter-add x16 -> x0, other arithmetic: 49.4 us -> none  [the longest x8 24.8 us: one_block(): totals = totals.at[left_safe].add(first_term)]
    gather x16 -> x0, local copies, waits for them, and re-layouts: 45.4 us -> none  [the longest x8 22.7 us: one_block(): right_rows = gathered[right_safe].astype(jnp.float32)]
    all_gather x1 -> x4, waiting for transfers between devices: 85.3 us -> 58.8 us  [the longest x1 26 us: local(): lax.all_gather(lax.ppermute(own, ('z', 'y'), moves()), 'z', axis=0, tiled...]
  transfers between devices with their start and end apart: 18 -> 12, of which waited for: 18 -> 10; matrix products, arithmetic and copies ran while one was open for 0% -> 1% of each run, Pallas kernels for 0% -> 5%
where the time goes in v1:
time: 402 us; the launch traced here: 395 us
  waiting for transfers between devices  214 us (53%)
  Pallas kernels  85 us (21%)
  blocking collectives  59.8 us (15%)
  between operations  15.7 us (4%)
  starting transfers between devices  8.91 us (2%)
  local copies, waits for them, and re-layouts  6.69 us (2%)
  other arithmetic  4.34 us (1%)
    pallas_call x1, Pallas kernels, local(): pl.pallas_call(pairs_kernel, out_shape=(acc, acc), in_specs=smem_specs(2)...  56.5 us
    reduce_scatter x1, waiting for transfers between devices, local(): lax.psum_scatter(lacc.reshape(NX, NY, 512, 128), 'x', scatter_dimension=0...  52.8 us
    reduce_scatter x1, waiting for transfers between devices, local(): lax.psum_scatter(from_right[0], 'z', scatter_dimension=0, tiled=True)  40.5 us
    reduce_scatter x1, waiting for transfers between devices, local(): lax.psum_scatter(from_left[0], 'y', scatter_dimension=0, tiled=True)  30.8 us
    reduce_scatter x1, waiting for transfers between devices, local(): lax.psum_scatter(racc.reshape(2, NZ, 512, 128), 'core', scatter_dimension...  27.9 us
    all_gather x1, waiting for transfers between devices, local(): lax.all_gather(lax.ppermute(own, ('z', 'y'), moves()), 'z', axis=0, tiled...  26 us
    psum x1, blocking collectives, local(): over = lax.psum(over, ('y', 'core'))  23.9 us
    all_gather x1, blocking collectives, local(): lax.all_gather(own, 'y', axis=0, tiled=True)  22.2 us
  transfers between devices with their start and end apart: 12, of which 10 were waited for; matrix products, arithmetic and copies ran while one was open for 1% of the time, Pallas kernels for 5%

profile of v1, /device:TPU:1, one launch (start us, length us, event | category | flops | bytes accessed | tf_op | source)
XLA Modules:
  0.0 394.7 jit_solution(14380416526326747541)
XLA Ops:
  7.4 3.3 collective-permute-start
  10.7 1.2 collective-permute-done
  12.0 1.0 maximum_select_fusion.1
  14.5 22.2 %all_gather.19 = bf16[32,64,128]{2,1,0:T(8,128)(2,1)} all-gather(bf16[8,64,128]{2,1,0:T(8,128)(2,1)S(1)} %maximum_select_fusion.1), channel_id=1, replica_groups=mesh['z'=8,'x'=4,'y'=4,'core'=2] {'y'}, dimensions={0}, use_global_device_ids=true | all-gather | bytes 655360 | tf_op jit(solution)/shard_map/all_gather | solution.py:270
  36.7 26.0 %all-gather.8.cloned.1.call-done = bf16[64,64,128]{2,1,0:T(8,128)(2,1)} async-done(((bf16[8,64,128]{2,1,0:T(8,128)(2,1)}), bf16[64,64,128]{2,1,0:T(8,128)(2,1)}) %all-gather.8.cloned.1.call-update) | async-done | bytes 1048592 | tf_op jit(solution)/shard_map/all_gather | solution.py:271
  62.8 1.3 dynamic-slice
  65.7 13.8 %all-reduce = s32[1024]{0:T(1024)S(1)} all-reduce(s32[1024]{0:T(1024)S(1)} %fusion.12), channel_id=2, replica_groups=mesh['z'=8,'x'=4,'y'=4,'core'=2] {'z','x'}, use_global_device_ids=true, to_apply=%add | all-reduce | flops 1024 | bytes 8192
  80.2 18.4 %assign.1.tasks_ref = s32[17]{0:T(128)} custom-call(s32[1]{0:T(128)} %bitcast.1.me_ref, s32[32,32]{1,0:T(8,128)} %reshape.87.code_ref), custom_call_target="tpu_custom_call" | custom-call | tf_op jit(solution)/shard_map/assign/pallas_call | solution.py:276
  99.2 1.7 all-gather.6.cloned.1.call-done
  100.8 18.5 %all-gather.10.cloned.1.call-done = bf16[128,64,128]{2,1,0:T(8,128)(2,1)} async-done(((bf16[64,64,128]{2,1,0:T(8,128)(2,1)}), bf16[128,64,128]{2,1,0:T(8,128)(2,1)}) %all-gather.10.cloned.1.call-update) | async-done | bytes 2097168 | tf_op jit(solution)/shard_map/all_gather | solution.py:272
  119.4 1.6 copy-done
  121.0 1.6 copy-done.1
  123.3 56.5 %pairs.1 = (f32[4,2048,128]{2,1,0:T(8,128)}, f32[4,2048,128]{2,1,0:T(8,128)}) custom-call(s32[1]{0:T(128)} %bitcast.lane_ref, s32[17]{0:T(128)S(1)} %copy-done.5, bf16[4,2048,128]{2,1,0:T(8,128)(2,1)S(1)} %bitcast.19, bf16[4,2048,128]{2,1,0:T(8,128)(2,1)S(1)} %bitcast.20, bf16[256,256]{1,0:T(8,128)(2,1)S(1)} %copy-done.2, bf16[256,256]{1,0:T(8,128)(2,1)S(1)} %copy-done.3, ...), custom_call_target="tpu_custom_call" | custom-call | tf_op jit(solution)/shard_map/pairs/pallas_call | solution.py:287
  180.4 27.9 %reduce-scatter.9.cloned.1.call-done = f32[1,8,512,128]{3,2,1,0:T(8,128)} async-done(((f32[2,8,512,128]{3,2,1,0:T(8,128)}), f32[1,8,512,128]{3,2,1,0:T(8,128)}) %reduce-scatter.9.cloned.1.call-update) | async-done | bytes 2097168 | tf_op jit(solution)/shard_map/reduce_scatter | solution.py:308
  208.4 52.8 %reduce-scatter.5.cloned.1.call-done = f32[1,4,512,128]{3,2,1,0:T(8,128)} async-done(((f32[4,4,512,128]{3,2,1,0:T(8,128)}), f32[1,4,512,128]{3,2,1,0:T(8,128)}) %reduce-scatter.5.cloned.1.call-update) | async-done | bytes 1048592 | tf_op jit(solution)/shard_map/reduce_scatter | solution.py:306
  261.7 40.5 %reduce-scatter.11.cloned.1.call-done = f32[1,512,128]{2,1,0:T(8,128)} async-done(((f32[8,512,128]{2,1,0:T(8,128)}), f32[1,512,128]{2,1,0:T(8,128)}) %reduce-scatter.11.cloned.1.call-update) | async-done | bytes 262160 | tf_op jit(solution)/shard_map/reduce_scatter | solution.py:309
  302.3 1.6 collective-permute-start.2
  303.9 30.8 %reduce-scatter.7.cloned.1.call-done = f32[1,512,128]{2,1,0:T(8,128)} async-done(((f32[4,512,128]{2,1,0:T(8,128)}), f32[1,512,128]{2,1,0:T(8,128)}) %reduce-scatter.7.cloned.1.call-update) | async-done | bytes 262160 | tf_op jit(solution)/shard_map/reduce_scatter | solution.py:307
  335.7 3.0 collective-permute-start.3
  338.7 1.2 collective-permute-done.3
  340.8 12.5 %all-gather.12.cloned.1.call-done = bf16[32,8,64,128]{3,2,1,0:T(8,128)(2,1)} async-done(((bf16[1,8,64,128]{3,2,1,0:T(8,128)(2,1)}), bf16[32,8,64,128]{3,2,1,0:T(8,128)(2,1)}) %all-gather.12.cloned.1.call-update) | async-done | bytes 4194320 | tf_op jit(solution)/shard_map/all_gather | solution.py:273
  353.4 5.1 %overlap.1 = f32[32,2,128]{2,1,0:T(2,128)} custom-call(f32[512,128]{1,0:T(8,128)} %maximum_select_fusion.x_ref, bf16[32,512,128]{2,1,0:T(8,128)(2,1)} %bitcast.21), custom_call_target="tpu_custom_call" | custom-call | tf_op jit(solution)/shard_map/overlap/pallas_call | solution.py:314
  358.5 23.9 %psum.7.over_ref = f32[32,2,128]{2,1,0:T(2,128)} all-reduce(f32[32,2,128]{2,1,0:T(2,128)} %overlap.1), channel_id=1, replica_groups=mesh['z'=8,'x'=4,'y'=4,'core'=2] {'y','core'}, use_global_device_ids=true, to_apply=%region_4.5 | all-reduce | flops 8192 | bytes 65536 | tf_op jit(solution)/shard_map/psum | solution.py:322
  382.3 5.0 %project.1 = f32[512,128]{1,0:T(8,128)} custom-call(f32[512,128]{1,0:T(8,128)} %maximum_select_fusion.x_ref, bf16[32,512,128]{2,1,0:T(8,128)(2,1)} %bitcast.22, f32[32,2,128]{2,1,0:T(2,128)} %psum.7.over_ref), custom_call_target="tpu_custom_call" | custom-call | tf_op jit(solution)/shard_map/project/pallas_call | solution.py:323
  (47 shorter events, 7.7 us)
Async XLA Ops:
  7.4 112.0 %copy-start.2 = (bf16[256,256]{1,0:T(8,128)(2,1)S(1)}, bf16[256,256]{1,0:T(8,128)(2,1)}, u32[]{:S(2)}) copy-start(bf16[256,256]{1,0:T(8,128)(2,1)} %constant.107.clone.wz_ref) | copy-start | bytes 393220
  7.4 112.0 %copy-start.3 = (bf16[256,256]{1,0:T(8,128)(2,1)S(1)}, bf16[256,256]{1,0:T(8,128)(2,1)}, u32[]{:S(2)}) copy-start(bf16[256,256]{1,0:T(8,128)(2,1)} %constant.108.clone.wy_ref) | copy-start | bytes 393220
  7.4 112.0 %copy-start.4 = (bf16[128,128]{1,0:T(8,128)(2,1)S(1)}, bf16[128,128]{1,0:T(8,128)(2,1)}, u32[]{:S(2)}) copy-start(bf16[128,128]{1,0:T(8,128)(2,1)} %constant.109.clone.wx_ref) | copy-start | bytes 98308
  7.4 55.4 %all-gather.8.cloned.1.call-start = ((), (), s32[]{:S(2)}) async-start(), calls=%async_computation.5 | async-start | bytes 1179648 | tf_op jit(solution)/shard_map/all_gather | solution.py:271
  7.4 4.5 %collective-permute-start = (bf16[8,64,128]{2,1,0:T(8,128)(2,1)}, bf16[8,64,128]{2,1,0:T(8,128)(2,1)S(1)}, u32[]{:S(2)}, u32[]{:S(2)}) collective-permute-start(bf16[8,64,128]{2,1,0:T(8,128)(2,1)} %bitcast.27), channel_id=1, source_target_pairs={{0,1},{1,0},{2,3},{3,2},{4,5},{5,4},{6,7},{7,6},{8,9},{9,8},{10,11... | collective-permute-start | bytes 393224 | tf_op jit(solution)/shard_map/ppermute | solution.py:254
  13.0 0.7 collective-permute-start.1
  13.7 0.7 copy-start.6
  14.4 86.4 %all-gather.6.cloned.1.call-start = ((), (), s32[]{:S(2)}) async-start(), calls=%async_computation.4 | async-start | bytes 2621440 | tf_op jit(solution)/shard_map/all_gather | solution.py:270
  36.7 82.7 %all-gather.10.cloned.1.call-start = ((), (), s32[]{:S(2)}) async-start(), calls=%async_computation.6 | async-start | bytes 3145728 | tf_op jit(solution)/shard_map/all_gather | solution.py:272
  62.8 145.5 %reduce-scatter.9.cloned.1.call-start = ((), (), s32[]{:S(2)}) async-start(), calls=%async_computation.9 | async-start | bytes 6291456 | tf_op jit(solution)/shard_map/reduce_scatter | solution.py:308
  119.4 1.6 copy-start
  121.0 1.6 copy-start.1
  122.6 0.7 copy-start.5
  179.8 81.4 %reduce-scatter.5.cloned.1.call-start = ((), (), s32[]{:S(2)}) async-start(), calls=%async_computation.7 | async-start | bytes 5242880 | tf_op jit(solution)/shard_map/reduce_scatter | solution.py:306
  180.4 121.9 %reduce-scatter.11.cloned.1.call-start = ((), (), s32[]{:S(2)}) async-start(), calls=%async_computation.10 | async-start | bytes 2359296 | tf_op jit(solution)/shard_map/reduce_scatter | solution.py:309
  208.3 126.3 %reduce-scatter.7.cloned.1.call-start = ((), (), s32[]{:S(2)}) async-start(), calls=%async_computation.8 | async-start | bytes 1310720 | tf_op jit(solution)/shard_map/reduce_scatter | solution.py:307
  261.2 92.2 %all-gather.12.cloned.1.call-start = ((), (), s32[]{:S(2)}) async-start(), calls=%async_computation.11 | async-start | bytes 4325376 | tf_op jit(solution)/shard_map/all_gather | solution.py:273
  302.3 32.4 %collective-permute-start.2 = (f32[1,512,128]{2,1,0:T(8,128)}, f32[1,512,128]{2,1,0:T(8,128)S(1)}, u32[]{:S(2)}, u32[]{:S(2)}) collective-permute-start(f32[1,512,128]{2,1,0:T(8,128)} %reduce-scatter.11.cloned.1.call-done), channel_id=1, source_target_pairs={{0,0},{32,2},{64,4},{96,6},{128,32},{160,34},{192,36},{224,38},{2,... | collective-permute-start | bytes 786440 | tf_op jit(solution)/shard_map/ppermute | solution.py:310
  335.7 4.2 %collective-permute-start.3 = (f32[512,128]{1,0:T(8,128)S(1)}, f32[512,128]{1,0:T(8,128)S(1)}, u32[]{:S(2)}, u32[]{:S(2)}) collective-permute-start(f32[512,128]{1,0:T(8,128)S(1)} %add_bitcast_fusion), channel_id=1, source_target_pairs={{0,1},{1,0},{2,3},{3,2},{4,5},{5,4},{6,7},{7,6},{8,9},{9,8},{10,11... | collective-permute-start | bytes 786440 | tf_op jit(solution)/shard_map/ppermute | solution.py:254
Sparse Core Ops, SparseCore 0:
  14.5 48.1 all-gather.7
  64.6 36.2 all-gather.5
  102.7 16.6 all-gather.9
  179.9 28.3 reduce-scatter.8
  210.9 50.2 reduce-scatter.4
  263.5 38.6 reduce-scatter.10
  304.8 29.7 reduce-scatter.6
Sparse Core Ops, SparseCore 1:
  264.6 88.7 all-gather.11
